TPU v7x, 256 devices: a whole 4x4x8 slice. The times are simulated.
256 devices in a mesh: segment: 32 (over z, x_lo, core), fsdp: 8 (over y, x_hi).
Axes of the slice: x: 4 (x_hi: 2, x_lo: 2; x = x_hi * 2 + x_lo), y: 4, z: 8, core: 2. Of those that a mesh axis runs over, the one named last changes fastest.
Arguments:
- new_batches: bfloat16 [3, 128, 4096], P(None, 'fsdp'), may hold values from -6 to 6
- down_state: bfloat16 [32, 128, 4096], P('segment', 'fsdp'), may hold values from -6 to 6
- up_state: bfloat16 [32, 128, 4096], P('segment', 'fsdp'), may hold values from -6 to 6
- gains: float32 [32, 2, 4096], P('segment'), may hold values from 0.1 to 1.9
- w_value: bfloat16 [32, 2, 4096, 1024], P('segment', None, None, 'fsdp'), may hold values from -0.09375 to 0.09375
- w_out: bfloat16 [32, 2, 1024, 4096], P('segment', None, 'fsdp'), may hold values from -0.1875 to 0.1875
- final_gain: float32 [4096], replicated, may hold values from 0.1 to 1.9
- lm_head: bfloat16 [4096, 131072], P(None, ('segment', 'fsdp')), may hold values from -12 to 12
- teacher_logits: bfloat16 [384, 131072], P(None, ('segment', 'fsdp')), may hold values from -100 to 300
Outputs:
- down_final: bfloat16 [32, 128, 4096], P('segment', 'fsdp')
- up_final: bfloat16 [32, 128, 4096], P('segment', 'fsdp')
- student_logits: bfloat16 [384, 131072], P(None, ('segment', 'fsdp'))
- divergence: float32 [384], replicated
All inputs are finite; a program needn't handle non-finite values.
Results may differ from a plain program's by a relative error of at most 0.028.
Values may be sent and summed in bfloat16 or wider, within the bound.
A program may use at most 64 MiB of HBM per device.

v0:
```python
import jax
import jax.numpy as jnp
from jax import lax
from jax.sharding import PartitionSpec as P

epsilon = 1e-06


def from_behind(value, axis, steps):
    count = lax.axis_size(axis)
    first, last = (max(0, -steps), min(count, count - steps))
    return lax.ppermute(value, axis, [(source, source + steps) for source in range(first, last)])


def from_root(value, axis, source):
    kept = jnp.where(lax.axis_index(axis) == source, value, 0).astype(value.dtype)
    return lax.psum(kept, axis)


def rms_scale(values, gain_row):
    return (
        values * lax.rsqrt(jnp.mean(values * values, axis=-1, keepdims=True) + epsilon) * gain_row
    )


def project_rows(inputs, gain_row, value_proj, out_proj):
    normed = rms_scale(inputs.astype(jnp.float32), gain_row).astype(jnp.bfloat16)
    head_values = jnp.dot(normed, value_proj, preferred_element_type=jnp.float32).astype(
        jnp.bfloat16
    )
    return jnp.dot(head_values, out_proj, preferred_element_type=jnp.float32)


def local(
    new_batches, down_state, up_state, gains, w_value, w_out, final_gain, lm_head, teacher_logits
):
    segment_index = lax.axis_index("segment")
    last_segment = lax.axis_size("segment") - 1
    ticks = new_batches.shape[0]
    gain_pair = gains[0]
    value_pair = w_value[0]
    out_pair = w_out[0]
    finished = []
    down_rows, up_rows, batches = (
        lax.all_gather(down_state[0], "fsdp", axis=0, tiled=True),
        lax.all_gather(up_state[0], "fsdp", axis=0, tiled=True),
        lax.all_gather(new_batches, "fsdp", axis=1, tiled=True),
    )
    for tick_index in range(ticks):
        down_sum, up_sum = (
            lax.psum(
                project_rows(down_rows, gain_pair[0], value_pair[0], out_pair[0]).astype(
                    jnp.bfloat16
                ),
                "fsdp",
            ).astype(jnp.float32),
            lax.psum(
                project_rows(up_rows, gain_pair[1], value_pair[1], out_pair[1]).astype(
                    jnp.bfloat16
                ),
                "fsdp",
            ).astype(jnp.float32),
        )
        out_down = (down_rows.astype(jnp.float32) + down_sum).astype(jnp.bfloat16)
        out_up = (up_rows.astype(jnp.float32) + up_sum).astype(jnp.bfloat16)
        moved_down = from_behind(out_down, "segment", 1)
        moved_up = from_behind(out_up, "segment", -1)
        down_rows = jnp.where(segment_index == 0, batches[tick_index], moved_down)
        up_rows = jnp.where(segment_index == last_segment, out_down, moved_up)
        finished.append(out_up)
    shard_rows = down_state.shape[1]
    replica = lax.axis_index("fsdp")
    down_final = lax.dynamic_slice_in_dim(down_rows, replica * shard_rows, shard_rows, 0)[None]
    up_final = lax.dynamic_slice_in_dim(up_rows, replica * shard_rows, shard_rows, 0)[None]
    stacked = jnp.concatenate(finished, axis=0)
    normed = rms_scale(stacked.astype(jnp.float32), final_gain).astype(jnp.bfloat16)
    hidden = from_root(normed, "segment", 0)
    logits = jnp.dot(hidden, lm_head, preferred_element_type=jnp.float32)
    teacher = teacher_logits.astype(jnp.float32)
    teach_max = jnp.max(teacher, axis=-1)
    teach_exp = jnp.exp(teacher - teach_max[:, None])
    teach_sum = jnp.sum(teach_exp, axis=-1)
    cross_sum = jnp.sum(teach_exp * (teacher - logits), axis=-1)
    stud_max = jnp.max(logits, axis=-1)
    stud_sum = jnp.sum(jnp.exp(logits - stud_max[:, None]), axis=-1)
    global_teach, global_stud = lax.pmax((teach_max, stud_max), ("segment", "fsdp"))
    teach_scale = jnp.exp(teach_max - global_teach)
    teach_sum, cross_sum, stud_sum = lax.psum(
        (
            teach_sum * teach_scale,
            cross_sum * teach_scale,
            stud_sum * jnp.exp(stud_max - global_stud),
        ),
        ("segment", "fsdp"),
    )
    teach_max = global_teach
    stud_max = global_stud
    divergence = (
        cross_sum / teach_sum - teach_max - jnp.log(teach_sum) + stud_max + jnp.log(stud_sum)
    )
    return (down_final, up_final, logits.astype(jnp.bfloat16), divergence)


def solution(mesh):
    placed = (
        P(None, "fsdp", None),
        P("segment", "fsdp", None),
        P("segment", "fsdp", None),
        P("segment", None, None),
        P("segment", None, None, "fsdp"),
        P("segment", None, "fsdp", None),
        P(),
        P(None, ("segment", "fsdp")),
        P(None, ("segment", "fsdp")),
    )
    return jax.shard_map(
        local,
        mesh=mesh,
        in_specs=placed,
        out_specs=(
            P("segment", "fsdp", None),
            P("segment", "fsdp", None),
            P(None, ("segment", "fsdp")),
            P(),
        ),
        check_vma=False,
    )
```

profile of v0, /device:TPU:1, one launch (start us, length us, event | category | flops | bytes accessed | tf_op | source)
XLA Modules:
  0.0 988.8 jit_solution(12093236995560547029)
XLA Ops:
  7.2 0.0 all-gather.8.cloned.1.call-start
  7.2 0.7 all-gather.8.cloned.1.call-update
  7.9 0.0 all-gather.10.cloned.1.call-start
  7.9 0.7 all-gather.10.cloned.1.call-update
  8.6 0.0 all-reduce.16.cloned.1.call-start
  8.7 0.9 fusion.118
  9.6 54.9 %all-gather.8.cloned.1.call-done = bf16[1,128,4096]{2,1,0:T(8,128)(2,1)} async-done(((bf16[1,16,4096]{2,1,0:T(8,128)(2,1)}), bf16[1,128,4096]{2,1,0:T(8,128)(2,1)}) %all-gather.8.cloned.1.call-update) | async-done | bytes 1048592 | tf_op jit(solution)/shard_map/all_gather | solution.py:45
  64.4 1.6 fusion.20
  66.1 51.3 %all-gather.10.cloned.1.call-done = bf16[1,128,4096]{2,1,0:T(8,128)(2,1)} async-done(((bf16[1,16,4096]{2,1,0:T(8,128)(2,1)}), bf16[1,128,4096]{2,1,0:T(8,128)(2,1)}) %all-gather.10.cloned.1.call-update) | async-done | bytes 1048592 | tf_op jit(solution)/shard_map/all_gather | solution.py:46
  117.4 1.5 fusion.24
  118.9 0.0 copy-start.2
  118.9 3.5 convolution_convert_fusion.5
  122.4 3.4 convolution_convert_fusion.2
  125.8 0.0 all-reduce.16.cloned.1.call-update
  125.9 0.0 all-gather.6.cloned.1.call-start
  125.9 0.5 all-gather.6.cloned.1.call-update
  126.5 0.0 all-reduce.14.cloned.1.call-start
  126.5 112.1 %all-reduce.16.cloned.1.call-done = (bf16[128,4096]{1,0:T(8,128)(2,1)}, bf16[128,4096]{1,0:T(8,128)(2,1)}) async-done(((bf16[128,4096]{1,0:T(8,128)(2,1)}, bf16[128,4096]{1,0:T(8,128)(2,1)}), (bf16[128,4096]{1,0:T(8,128)(2,1)}, bf16[128,4096]{1,0:T(8,128)(2,1)})) %all-reduce.16.cloned.1.call-update) | async-done | bytes 2097168 | tf_op jit(solution)/shard_map/psum | solution.py:51
  238.6 1.5 fusion.27
  240.1 2.8 collective-permute-start.3
  242.9 16.1 %collective-permute-done.3 = bf16[128,4096]{1,0:T(8,128)(2,1)S(1)} collective-permute-done((bf16[128,4096]{1,0:T(8,128)(2,1)S(1)}, bf16[128,4096]{1,0:T(8,128)(2,1)S(1)}, u32[]{:S(2)}, u32[]{:S(2)}) %collective-permute-start.3) | collective-permute-done | bytes 1048608 | tf_op jit(solution)/shard_map/ppermute | solution.py:12
  259.0 3.1 fusion.12
  262.1 1.9 collective-permute-start
  264.1 3.4 convolution_convert_fusion.1
  267.5 39.8 %all-gather.6.cloned.1.call-done = bf16[3,128,4096]{2,1,0:T(8,128)(2,1)} async-done(((bf16[3,16,4096]{2,1,0:T(8,128)(2,1)}), bf16[3,128,4096]{2,1,0:T(8,128)(2,1)}) %all-gather.6.cloned.1.call-update) | async-done | bytes 3145744 | tf_op jit(solution)/shard_map/all_gather | solution.py:47
  307.3 0.0 collective-permute-done
  307.3 2.0 fusion.4
  309.3 3.8 convolution_convert_fusion.4
  313.1 0.0 all-reduce.14.cloned.1.call-update
  313.1 0.0 all-reduce.12.cloned.1.call-start
  313.2 110.8 %all-reduce.14.cloned.1.call-done = (bf16[128,4096]{1,0:T(8,128)(2,1)}, bf16[128,4096]{1,0:T(8,128)(2,1)}) async-done(((bf16[128,4096]{1,0:T(8,128)(2,1)}, bf16[128,4096]{1,0:T(8,128)(2,1)}), (bf16[128,4096]{1,0:T(8,128)(2,1)}, bf16[128,4096]{1,0:T(8,128)(2,1)})) %all-reduce.14.cloned.1.call-update) | async-done | bytes 2097168 | tf_op jit(solution)/shard_map/psum | solution.py:51
  424.0 1.6 fusion.15
  425.5 2.8 collective-permute-start.4
  428.3 13.3 %collective-permute-done.4 = bf16[128,4096]{1,0:T(8,128)(2,1)S(1)} collective-permute-done((bf16[128,4096]{1,0:T(8,128)(2,1)S(1)}, bf16[128,4096]{1,0:T(8,128)(2,1)S(1)}, u32[]{:S(2)}, u32[]{:S(2)}) %collective-permute-start.4) | collective-permute-done | bytes 1048608 | tf_op jit(solution)/shard_map/ppermute | solution.py:12
  441.6 2.8 fusion.16
  444.4 1.9 collective-permute-start.1
  446.4 3.4 convolution_convert_fusion
  449.8 8.6 collective-permute-done.1
  458.4 2.0 fusion.8
  460.4 3.8 convolution_convert_fusion.3
  464.2 0.0 all-reduce.12.cloned.1.call-update
  464.3 0.0 all-reduce.10.cloned.1.call-start
  464.3 114.7 %all-reduce.12.cloned.1.call-done = (bf16[128,4096]{1,0:T(8,128)(2,1)}, bf16[128,4096]{1,0:T(8,128)(2,1)}) async-done(((bf16[128,4096]{1,0:T(8,128)(2,1)}, bf16[128,4096]{1,0:T(8,128)(2,1)}), (bf16[128,4096]{1,0:T(8,128)(2,1)}, bf16[128,4096]{1,0:T(8,128)(2,1)})) %all-reduce.12.cloned.1.call-update) | async-done | bytes 2097168 | tf_op jit(solution)/shard_map/psum | solution.py:51
  579.0 1.8 fusion.19
  580.8 0.0 copy-start.8
  580.8 0.8 fusion
  581.6 2.3 fusion.3
  583.9 0.0 all-reduce.10.cloned.1.call-update
  584.0 1.0 copy-done.6
  584.9 0.1 reduce_max.23
  585.1 2.8 collective-permute-start.5
  587.9 1.5 fusion.11
  589.3 3.0 collective-permute-start.2
  592.3 1.3 slice_bitcast_fusion.2
  593.6 9.2 collective-permute-done.5
  602.7 0.7 fusion.110
  603.4 13.3 %collective-permute-done.2 = bf16[128,4096]{1,0:T(8,128)(2,1)S(1)} collective-permute-done((bf16[128,4096]{1,0:T(8,128)(2,1)S(1)}, bf16[128,4096]{1,0:T(8,128)(2,1)S(1)}, u32[]{:S(2)}, u32[]{:S(2)}) %collective-permute-start.2) | collective-permute-done | bytes 1048608 | tf_op jit(solution)/shard_map/ppermute | solution.py:12
  616.7 0.7 fusion.111
  617.4 207.1 %all-reduce.10.cloned.1.call-done = bf16[384,4096]{1,0:T(8,128)(2,1)} async-done(((bf16[384,4096]{1,0:T(8,128)(2,1)}), bf16[384,4096]{1,0:T(8,128)(2,1)}) %all-reduce.10.cloned.1.call-update) | async-done | bytes 3145744 | tf_op jit(solution)/shard_map/psum | solution.py:17
  824.5 5.0 fusion.119
  829.5 77.8 %all-reduce.1 = (f32[384]{0:T(512)S(1)}, f32[384]{0:T(512)S(1)}) all-reduce(f32[384]{0:T(512)S(1)} %get-tuple-element.33, bf16[384]{0:T(512)(128)(2,1)S(1)} %reduce_max.23), channel_id=1, replica_groups=mesh['segment'=32,'fsdp'=8] {'segment','fsdp'}, use_global_device_ids=true, to_apply=%region_21.22 | all-reduce | flops 768 | bytes 5376 | tf_op jit(solution)/shard_map/pmax | solution.py:86
  907.3 1.3 fusion.109
  908.7 72.7 %all-reduce = (f32[384]{0:T(512)S(1)}, f32[384]{0:T(512)S(1)}, f32[384]{0:T(512)S(1)}) all-reduce(f32[384]{0:T(512)S(1)} %get-tuple-element.35, f32[384]{0:T(512)S(1)} %get-tuple-element.32, f32[384]{0:T(512)S(1)} %get-tuple-element.31), channel_id=1, replica_groups=mesh['segment'=32,'fsdp'=8] {'segment','fsdp'}, use_global_device_ids=true, to_apply=%region_23.24 | all-reduce | flops 1152 | bytes 9216 | tf_op jit(solution)/shard_map/psum | solution.py:88
  981.4 0.6 log_add_fusion
  (24 shorter events, 0.1 us)
Async XLA Ops:
  7.2 57.3 %all-gather.8.cloned.1.call-start = ((), (), s32[]{:S(2)}) async-start(), calls=%async_computation.2 | async-start | bytes 1179648 | tf_op jit(solution)/shard_map/all_gather | solution.py:45
  7.9 109.5 %all-gather.10.cloned.1.call-start = ((), (), s32[]{:S(2)}) async-start(), calls=%async_computation.3 | async-start | bytes 1179648 | tf_op jit(solution)/shard_map/all_gather | solution.py:46
  8.6 230.0 %all-reduce.16.cloned.1.call-start = ((), (), s32[]{:S(2)}) async-start(), calls=%async_computation.6 | async-start | bytes 4194304 | tf_op jit(solution)/shard_map/psum | solution.py:51
  64.4 54.5 %copy-start.4 = (bf16[1,128,4096]{2,1,0:T(8,128)(2,1)S(1)}, bf16[1,128,4096]{2,1,0:T(8,128)(2,1)}, u32[]{:S(2)}) copy-start(bf16[1,128,4096]{2,1,0:T(8,128)(2,1)} %all-gather.8.cloned.1.call-done) | copy-start | bytes 3145732
  118.9 3.5 copy-start.2
  125.9 181.4 %all-gather.6.cloned.1.call-start = ((), (), s32[]{:S(2)}) async-start(), calls=%async_computation | async-start | bytes 3538944 | tf_op jit(solution)/shard_map/all_gather | solution.py:47
  126.5 297.5 %all-reduce.14.cloned.1.call-start = ((), (), s32[]{:S(2)}) async-start(), calls=%async_computation.5 | async-start | bytes 4194304 | tf_op jit(solution)/shard_map/psum | solution.py:51
  240.1 18.9 %collective-permute-start.3 = (bf16[128,4096]{1,0:T(8,128)(2,1)S(1)}, bf16[128,4096]{1,0:T(8,128)(2,1)S(1)}, u32[]{:S(2)}, u32[]{:S(2)}) collective-permute-start(bf16[128,4096]{1,0:T(8,128)(2,1)S(1)} %fusion.27), channel_id=1, source_target_pairs={{8,0},{16,8},{24,16},{32,24},{40,32},{48,40},{56,48},{64,56},{72,6... | collective-permute-start | bytes 3145736 | tf_op jit(solution)/shard_map/ppermute | solution.py:12
  262.1 45.2 %collective-permute-start = (bf16[128,4096]{1,0:T(8,128)(2,1)}, bf16[128,4096]{1,0:T(8,128)(2,1)}, u32[]{:S(2)}, u32[]{:S(2)}) collective-permute-start(bf16[128,4096]{1,0:T(8,128)(2,1)} %get-tuple-element.25), channel_id=1, source_target_pairs={{0,8},{8,16},{16,24},{24,32},{32,40},{40,48},{48,56},{56,64},{64,7... | collective-permute-start | bytes 3145736 | tf_op jit(solution)/shard_map/ppermute | solution.py:12
  309.3 3.8 copy-start.5
  313.1 265.9 %all-reduce.12.cloned.1.call-start = ((), (), s32[]{:S(2)}) async-start(), calls=%async_computation.4 | async-start | bytes 4194304 | tf_op jit(solution)/shard_map/psum | solution.py:51
  424.0 17.7 %copy-start.7 = (bf16[128,4096]{1,0:T(8,128)(2,1)S(1)}, bf16[128,4096]{1,0:T(8,128)(2,1)}, u32[]{:S(2)}) copy-start(bf16[128,4096]{1,0:T(8,128)(2,1)} %get-tuple-element.14) | copy-start | bytes 3145732
  425.5 16.1 %collective-permute-start.4 = (bf16[128,4096]{1,0:T(8,128)(2,1)S(1)}, bf16[128,4096]{1,0:T(8,128)(2,1)S(1)}, u32[]{:S(2)}, u32[]{:S(2)}) collective-permute-start(bf16[128,4096]{1,0:T(8,128)(2,1)S(1)} %fusion.15), channel_id=1, source_target_pairs={{8,0},{16,8},{24,16},{32,24},{40,32},{48,40},{56,48},{64,56},{72,6... | collective-permute-start | bytes 3145736 | tf_op jit(solution)/shard_map/ppermute | solution.py:12
  444.4 5.3 copy-start.3
  444.4 14.0 %collective-permute-start.1 = (bf16[128,4096]{1,0:T(8,128)(2,1)}, bf16[128,4096]{1,0:T(8,128)(2,1)}, u32[]{:S(2)}, u32[]{:S(2)}) collective-permute-start(bf16[128,4096]{1,0:T(8,128)(2,1)} %get-tuple-element.20), channel_id=1, source_target_pairs={{0,8},{8,16},{16,24},{24,32},{32,40},{40,48},{48,56},{56,64},{64,7... | collective-permute-start | bytes 3145736 | tf_op jit(solution)/shard_map/ppermute | solution.py:12
  460.4 3.8 copy-start
  464.3 360.3 %all-reduce.10.cloned.1.call-start = ((), (), s32[]{:S(2)}) async-start(), calls=%async_computation.1 | async-start | bytes 6291456 | tf_op jit(solution)/shard_map/psum | solution.py:17
  580.8 0.8 copy-start.8
  583.9 1.0 copy-start.6
  583.9 3.9 copy-start.1
  585.1 17.7 %collective-permute-start.5 = (bf16[128,4096]{1,0:T(8,128)(2,1)S(1)}, bf16[128,4096]{1,0:T(8,128)(2,1)S(1)}, u32[]{:S(2)}, u32[]{:S(2)}) collective-permute-start(bf16[128,4096]{1,0:T(8,128)(2,1)S(1)} %fusion.19), channel_id=1, source_target_pairs={{8,0},{16,8},{24,16},{32,24},{40,32},{48,40},{56,48},{64,56},{72,6... | collective-permute-start | bytes 3145736 | tf_op jit(solution)/shard_map/ppermute | solution.py:12
  589.3 27.4 %collective-permute-start.2 = (bf16[128,4096]{1,0:T(8,128)(2,1)S(1)}, bf16[128,4096]{1,0:T(8,128)(2,1)S(1)}, u32[]{:S(2)}, u32[]{:S(2)}) collective-permute-start(bf16[128,4096]{1,0:T(8,128)(2,1)S(1)} %fusion.11), channel_id=1, source_target_pairs={{0,8},{8,16},{16,24},{24,32},{32,40},{40,48},{48,56},{56,64},{64,7... | collective-permute-start | bytes 3145736 | tf_op jit(solution)/shard_map/ppermute | solution.py:12
Sparse Core Ops, SparseCore 0:
  10.6 53.7 all-gather.7
  67.1 50.2 all-gather.9
  126.0 112.5 all-reduce.15
  241.1 66.1 all-gather.5
  313.3 110.6 all-reduce.13
  464.4 114.5 all-reduce.11
  584.1 240.4 all-reduce.9
where the time goes:
time: 990 us; the launch traced here: 989 us
  waiting for transfers between devices  753 us (76%)
  blocking collectives  150 us (15%)
  matrix products  26.3 us (3%)
  other arithmetic  25.9 us (3%)
  starting transfers between devices  15.4 us (2%)
  between operations  14.3 us (1%)
    psum x3, waiting for transfers between devices, local(): lax.psum(project_rows(down_rows, gain_pair[0], value_pair[0], out_pair[0]...  338 us
    psum x1, waiting for transfers between devices, from_root(): return lax.psum(kept, axis)  207 us
    pmax x1, blocking collectives, local(): lax.pmax((teach_max, stud_max), ('segment', 'fsdp'))  77.8 us
    psum x1, blocking collectives, local(): lax.psum((teach_sum * teach_scale, cross_sum * teach_scale, stud_sum * jn...  72.7 us
    ppermute x6, waiting for transfers between devices, from_behind(): lax.ppermute(value, axis, [(source, source + steps) for source in range(f...  60.5 us
    all_gather x1, waiting for transfers between devices, local(): lax.all_gather(down_state[0], 'fsdp', axis=0, tiled=True)  54.9 us
    all_gather x1, waiting for transfers between devices, local(): lax.all_gather(up_state[0], 'fsdp', axis=0, tiled=True)  51.3 us
    all_gather x1, waiting for transfers between devices, local(): lax.all_gather(new_batches, 'fsdp', axis=1, tiled=True)  39.8 us
  transfers between devices with their start and end apart: 13, of which 12 were waited for; matrix products, arithmetic and copies ran while one was open for 2% of the time, Pallas kernels for 0%

commit v1 on v0

v1 whole, which is shorter than its diff:
```python
import functools

import jax
import jax.numpy as jnp
from jax import lax
from jax.experimental import pallas as pl
from jax.experimental.pallas import tpu as pltpu
from jax.sharding import PartitionSpec as P

MESH = pl.DeviceIdType.MESH
BF = jnp.bfloat16
F32 = jnp.float32
EPS = 1e-06

D = 4096
H = 1024
FS = 8
SEG = 32
MB = 128
TICKS = 3
ROWS = MB // FS
COLS = D // FS
WIDE = H + 128
VOC = 512
DOWN, UP = 0, 1
VMEM_LIMIT = 64 * 1024 * 1024 - 65536

(SEND_DOWN, SEND_UP, HEAD, REDUCE, OUT, FORWARD, SHARE, LOGITS, MERGE, FINISH, SPREAD, NOTHING) = range(12)


def step(kind, section=0, tick=0):
    return kind * 8 + section * 4 + tick


def parse(words):
    names = {
        "W": SEND_DOWN, "V": SEND_UP, "A": HEAD, "B": REDUCE, "C": OUT, "D": FORWARD, "E": SHARE,
        "F": LOGITS, "G": MERGE, "H": FINISH, "I": SPREAD,
    }
    steps = []
    for word in words:
        section, tick = 0, 0
        for mark in word[1:]:
            if mark in "du":
                section = "du".index(mark)
            else:
                tick = int(mark)
        steps.append((names[word[0]], section, tick))
    return steps


FIRST = (
    "Vu0", "Au0", "Vu1", "Vu2", "Vu3", "Wd0", "Bu0", "Wd1", "Cd0", "D0", "Cu0", "Au1",
    "Wd2", "Wd3", "Bu1", "Wu0", "Cd1", "D1", "Cu1", "Au2", "Wu1", "Wu2", "Bu2", "Wu3",
    "Ad0", "Cd2", "D2", "Ad1", "E0", "Bd0", "Bd1", "F0", "Ad2", "E1", "Bd2", "F1",
    "Cu2", "Iu", "Id", "E2", "F2", "G0", "G1", "G2", "H0", "H1", "H2",
)
MIDDLE = (
    "Vu0", "Au0", "Vu1", "Vu2", "Vu3", "Wd0", "Bu0", "Wd1", "Cu0", "Au1", "Wd2", "Wd3",
    "Bu1", "Wu0", "Wu1", "Wu2", "Wu3", "D0", "Ad0", "E0", "Bd0", "D1", "Cd0", "Ad1",
    "Cu1", "Au2", "E1", "F0", "Bd1", "Bu2", "D2", "Cd1", "Ad2", "Cu2", "E2", "F1",
    "Bd2", "F2", "Cd2", "Iu", "Id", "G0", "G1", "G2", "H0", "H1", "H2",
)
LAST = (
    "Vu0", "Au0", "Vu1", "Vu2", "Vu3", "Wd0", "Bu0", "Wd1", "Wd2", "Wd3", "Wu0", "Wu1",
    "Wu2", "Wu3", "D0", "Ad0", "E0", "Bd0", "Cu0", "Au1", "D1", "Cd0", "Ad1", "Bu1",
    "E1", "Bd1", "Cu1", "Au2", "F0", "Cd1", "Ad2", "Bu2", "Bd2", "D2", "F1", "Cu2",
    "Iu", "E2", "Cd2", "Id", "F2", "G0", "G1", "G2", "H0", "H1", "H2",
)
TABLES = [parse(FIRST), parse(MIDDLE), parse(LAST)]
STEPS = max(len(table) for table in TABLES)
TABLES = [table + [(NOTHING, 0, 0)] * (STEPS - len(table)) for table in TABLES]


def take(ref, sem):
    pltpu.make_async_copy(ref, ref, sem).wait()


def kernel(
    new_ref, down_ref, up_ref, gain_ref, value_ref, out_ref, final_ref, head_ref, teach_ref,
    down_out, up_out, logit_out, div_out,
    pw, ow, xb, xp, part, parts, hvo, hv, xo, hid, hn, acc, head, teach, cols, st1, st2, fin,
    gain, final, local_w, local_x, local_h,
    w_s, w_r, x_s, x_r, rs_s, rs_r, ag_s, ag_r, hop_s, hop_r, z_s, z_r, pl_s, pl_r, d2_s, d2_r,
    s1_s, s1_r, s2_s, s2_r, f_s, f_r,
):
    s = lax.axis_index("segment")
    f = lax.axis_index("fsdp")
    z, xl, c = lax.div(s, 4), lax.rem(lax.div(s, 2), 2), lax.rem(s, 2)
    y, xh = lax.div(f, 2), lax.rem(f, 2)
    x = xh * 2 + xl
    first, last = s == 0, s == SEG - 1
    frow = pl.multiple_of(f * ROWS, ROWS)
    fcol = pl.multiple_of(f * COLS, COLS)
    fhead = pl.multiple_of(f * 128, 128)
    quarter = c * 2 + xl
    qrow = pl.multiple_of(quarter * 32, 32)
    orow = pl.multiple_of((c * 2 + 1 - xl) * 32, 32)
    crow = pl.multiple_of(c * 64, 64)
    prow = pl.multiple_of((1 - c) * 64, 64)

    def follows(section):
        inside = jnp.where(section == DOWN, last, first)
        ahead = jnp.where(section == DOWN, 1, -1)
        return inside, s + jnp.where(inside, 0, ahead), jnp.where(inside, 1 - section, section)

    def plane(k):
        x2, y2 = lax.rem(x + lax.rem(k, 4), 4), lax.rem(y + lax.div(k, 4), 4)
        return x2, (z * 4 + lax.rem(x2, 2) * 2 + c, y2 * 2 + lax.div(x2, 2))

    def pillar(k):
        z2, c2 = lax.rem(z + lax.div(k, 2), 8), lax.rem(c + lax.rem(k, 2), 2)
        return (z2 * 4 + xl * 2 + c2, f)

    def put(src, dst, send, recv, target):
        pltpu.make_async_remote_copy(
            src_ref=src, dst_ref=dst, send_sem=send, recv_sem=recv,
            device_id=target, device_id_type=MESH,
        ).start()

    head_copy = pltpu.make_async_copy(head_ref, head, local_h.at[0])
    teach_copy = pltpu.make_async_copy(teach_ref, teach, local_h.at[1])
    gain_copy = pltpu.make_async_copy(gain_ref, gain, local_h.at[3])
    final_copy = pltpu.make_async_copy(final_ref, final, local_h.at[4])
    gain_copy.start()
    for i, state in enumerate((down_ref, up_ref)):
        pltpu.make_async_copy(
            state.at[0, :, pl.ds(fcol, COLS)], xb.at[i, 0, pl.ds(frow, ROWS), :], local_x.at[i]
        ).start()
    for i in range(2):
        pltpu.make_async_copy(
            value_ref.at[0, i, pl.ds(pl.multiple_of(f * COLS, COLS), COLS), :],
            pw.at[i, :, pl.ds(fhead, 128)], local_w.at[i],
        ).start()

        @pl.when(follows(i)[0])
        def _():
            pltpu.make_async_copy(
                out_ref.at[0, i, :, pl.ds(fcol, COLS)], ow.at[1 - i, pl.ds(fhead, 128), :],
                local_w.at[3 - i],
            ).start()

    barrier = pltpu.get_barrier_semaphore()

    def greet(target):
        pl.semaphore_signal(barrier, inc=1, device_id=target, device_id_type=MESH)

    @pl.loop(1, 16)
    def _(k):
        greet(plane(k)[1])
        greet(pillar(k))

    @pl.when(jnp.logical_not(first))
    def _():
        greet((0, f))

        @pl.loop(0, FS)
        def _(k):
            greet((s - 1, k))

    @pl.when(jnp.logical_not(last))
    def _():
        @pl.loop(0, FS)
        def _(k):
            greet((s + 1, k))

    @pl.when(first)
    def _():
        @pl.loop(1, SEG)
        def _(k):
            greet((k, f))

    pl.semaphore_wait(
        barrier, 30 + jnp.where(first, FS + SEG - 1, 2 * FS + 1) - jnp.where(last, FS, 0)
    )

    def send_states(i, state, lead, section, tick):
        for j in range(1, FS):
            p = lax.rem(f + j, FS)
            put(
                state.at[lead, :, pl.ds(pl.multiple_of(p * COLS, COLS), COLS)],
                xb.at[section, tick, pl.ds(frow, ROWS), :],
                x_s.at[i], x_r.at[i], (s, p),
            )

    def send_value(i, chunk):
        row = pl.multiple_of(chunk * 128, 128)
        for j in range(1, FS):
            p = lax.rem(f + j, FS)
            put(
                value_ref.at[0, i, pl.ds(pl.multiple_of(p * COLS + row, 128), 128), :],
                pw.at[i, pl.ds(row, 128), pl.ds(fhead, 128)], w_s.at[i], w_r.at[i], (s, p),
            )

    def send_out(i, chunk):
        inside, to, slot = follows(i)
        row = pl.multiple_of(chunk * 32, 32)
        for j in range(FS):
            p = lax.rem(f + j, FS)
            send = functools.partial(
                put,
                out_ref.at[0, i, pl.ds(row, 32), pl.ds(pl.multiple_of(p * COLS, COLS), COLS)],
                ow.at[slot, pl.ds(pl.multiple_of(f * 128 + row, 32), 32), :],
                w_s.at[2 + i], w_r.at[2 + slot], (to, p),
            )
            if j == 0:
                pl.when(jnp.logical_not(inside))(send)
            else:
                send()

    def do_send(i, what, chunk):
        pl.when(what == 0)(functools.partial(send_value, i, chunk))
        pl.when(what == 1)(functools.partial(send_out, i, chunk))

    send_states(UP, up_ref, 0, UP, 0)
    send_states(DOWN, down_ref, 0, DOWN, 0)

    @pl.loop(0, 4)
    def _(chunk):
        send_value(UP, chunk)

    head_copy.start()
    teach_copy.start()
    final_copy.start()

    @pl.when(first)
    def _():
        for i in range(2):
            pltpu.make_async_copy(
                new_ref.at[i, :, pl.ds(fcol, COLS)],
                xb.at[DOWN, 1 + i, pl.ds(frow, ROWS), :], local_x.at[2 + i],
            ).start()
            send_states(2 + i, new_ref, i, DOWN, 1 + i)

    gain_copy.wait()

    codes = []
    for i in range(STEPS):
        a, b, d = (step(*rows[i]) for rows in TABLES)
        codes.append(b if a == b == d else jnp.where(first, a, jnp.where(last, d, b)))

    def do_head(section, tick):
        @pl.when(tick == 0)
        def _():
            take(xb.at[section, 0, pl.ds(0, 112), :], x_r.at[section])
            take(xb.at[section, 0, pl.ds(0, ROWS), :], local_x.at[section])
            take(pw.at[section, :, pl.ds(0, 896)], w_r.at[section])
            take(pw.at[section, :, pl.ds(0, 128)], local_w.at[section])

        @pl.when(jnp.logical_and(tick > 0, jnp.logical_and(first, section == DOWN)))
        def _():
            take(xb.at[DOWN, tick, pl.ds(0, 112), :], x_r.at[1 + tick])
            take(xb.at[DOWN, tick, pl.ds(0, ROWS), :], local_x.at[1 + tick])

        rows = xb[section, tick].astype(F32)
        square = jnp.sum(rows * rows, axis=-1, keepdims=True)
        scaled = (rows * gain[0, pl.ds(section, 1), pl.ds(fcol, COLS)]).astype(BF)
        part[section, tick, :, 0:H] = jnp.dot(
            scaled, pw[section], preferred_element_type=F32
        ).astype(BF)
        high = square.astype(BF).astype(F32)
        lane = lax.broadcasted_iota(jnp.int32, (MB, 128), 1)
        part[section, tick, :, H:WIDE] = jnp.where(lane < 64, high, square - high).astype(BF)
        for j in range(1, FS):
            p = lax.rem(f + j, FS)
            put(
                part.at[section, tick, pl.ds(pl.multiple_of(p * ROWS, ROWS), ROWS), :],
                parts.at[section, tick, f], rs_s.at[section, tick], rs_r.at[section, tick], (s, p),
            )
        inside, to, slot = follows(section)

        @pl.when(inside)
        def _():
            xp[1 - section, tick] = xb[section, tick]

        @pl.when(jnp.logical_not(inside))
        def _():
            put(
                xb.at[section, tick], xp.at[section, tick],
                hop_s.at[section, tick], hop_r.at[section, tick], (to, f),
            )

    def do_reduce(section, tick):
        take(parts.at[section, tick, pl.ds(0, FS - 1)], rs_r.at[section, tick])
        total = part[section, tick, pl.ds(frow, ROWS), :].astype(F32)
        for j in range(1, FS):
            total = total + parts[section, tick, lax.rem(f + j, FS)].astype(F32)
        square = total[:, H : H + 1] + total[:, H + 64 : H + 65]
        scale = lax.rsqrt(square * (1.0 / D) + EPS)
        hvo[section, tick] = (total[:, 0:H] * scale).astype(BF)
        inside, to, slot = follows(section)
        for j in range(FS):
            p = lax.rem(f + j, FS)
            send = functools.partial(
                put, hvo.at[section, tick], hv.at[slot, tick, pl.ds(frow, ROWS), :],
                ag_s.at[section, tick], ag_r.at[slot, tick], (to, p),
            )
            if j == 0:
                pl.when(jnp.logical_not(inside))(send)
            else:
                send()

        @pl.when(inside)
        def _():
            hv[1 - section, tick, pl.ds(frow, ROWS), :] = hvo[section, tick]

    def do_out(slot, tick):
        within = jnp.where(slot == DOWN, first, last)

        @pl.when(within)
        def _():
            @pl.when(tick == 0)
            def _():
                take(ow.at[slot, pl.ds(0, 896), :], w_r.at[2 + slot])
                take(ow.at[slot, pl.ds(0, 128), :], local_w.at[2 + slot])

            take(hv.at[slot, tick, pl.ds(0, 112), :], ag_r.at[slot, tick])

        @pl.when(jnp.logical_not(within))
        def _():
            @pl.when(tick == 0)
            def _():
                take(ow.at[slot], w_r.at[2 + slot])

            take(xp.at[slot, tick], hop_r.at[slot, tick])
            take(hv.at[slot, tick], ag_r.at[slot, tick])

        added = jnp.dot(hv[slot, tick], ow[slot], preferred_element_type=F32)
        result = (xp[slot, tick].astype(F32) + added).astype(BF)
        done = jnp.logical_and(first, slot == DOWN)

        @pl.when(jnp.logical_not(done))
        def _():
            xb[slot, tick + 1] = result

        @pl.when(done)
        def _():
            xo[tick] = result
            hid[tick, 0:32, pl.ds(fcol, COLS)] = xo[tick, 0:32, :]

            @pl.loop(1, SEG)
            def _(k):
                to = 1 + lax.rem(k + 14, SEG - 1)
                piece = lax.rem(to, 2) * 2 + lax.rem(lax.div(to, 2), 2)
                row = pl.multiple_of(piece * 32, 32)
                put(
                    xo.at[tick, pl.ds(row, 32), :],
                    hid.at[tick, pl.ds(row, 32), pl.ds(fcol, COLS)],
                    z_s.at[tick, lax.div(to, 4)], z_r.at[tick], (to, f),
                )

    def do_forward(tick):
        mine = hid.at[tick, pl.ds(qrow, 32), pl.ds(fcol, COLS)]

        @pl.when(jnp.logical_not(first))
        def _():
            take(mine, z_r.at[tick])

        @pl.loop(1, 16)
        def _(k):
            x2, target = plane(k)
            other = lax.rem(x + x2, 2)
            put(mine, mine, pl_s.at[tick, other], pl_r.at[tick, other], target)

    def do_share(tick):
        take(hid.at[tick, pl.ds(qrow, 32), pl.ds(0, D - COLS)], pl_r.at[tick, 0])
        take(hid.at[tick, pl.ds(orow, 32), :], pl_r.at[tick, 1])
        half = hid.at[tick, pl.ds(crow, 64), :]
        put(half, half, d2_s.at[tick], d2_r.at[tick], (s + 1 - 2 * c, f))

    def do_logits(tick):
        @pl.when(tick == 0)
        def _():
            head_copy.wait()
            teach_copy.wait()
            final_copy.wait()

        take(hid.at[tick, pl.ds(prow, 64), :], d2_r.at[tick])

        @pl.loop(0, MB // 16)
        def _(i):
            row = pl.multiple_of(i * 16, 16)
            rows = hid[tick, pl.ds(row, 16), :].astype(F32)
            scale = lax.rsqrt(jnp.mean(rows * rows, axis=-1, keepdims=True) + EPS)
            hn[pl.ds(row, 16), :] = (rows * scale * final[...]).astype(BF)

        acc[...] = jnp.zeros_like(acc)

        @pl.loop(0, 4)
        def _(k):
            deep = pl.multiple_of(k * 1024, 1024)
            acc[...] += jnp.dot(
                hn[:, pl.ds(deep, 1024)], head[pl.ds(deep, 1024), :], preferred_element_type=F32
            )

        @pl.loop(0, 4)
        def _(i):
            row = pl.multiple_of(i * 32, 32)
            there = pl.multiple_of(tick * MB + i * 32, 32)
            logits = acc[pl.ds(row, 32), :]
            logit_out[pl.ds(there, 32), :] = logits.astype(BF)
            taught = teach[pl.ds(there, 32), :].astype(F32)
            teach_max = jnp.max(taught, axis=-1, keepdims=True)
            weight = jnp.exp(taught - teach_max)
            teach_sum = jnp.sum(weight, axis=-1, keepdims=True)
            cross = jnp.sum(weight * (taught - logits), axis=-1, keepdims=True)
            stud_max = jnp.max(logits, axis=-1, keepdims=True)
            stud_sum = jnp.sum(jnp.exp(logits - stud_max), axis=-1, keepdims=True)
            lane = lax.broadcasted_iota(jnp.int32, (32, 128), 1)
            packed = jnp.where(lane == 0, teach_max, stud_max)
            packed = jnp.where(lane == 1, teach_sum, packed)
            packed = jnp.where(lane == 2, cross, packed)
            packed = jnp.where(lane == 4, stud_sum, packed)
            cols[pl.ds(row, 32), :] = packed

        slot = x * 4 + y
        st1[tick, slot] = cols[...].T[0:8, :]
        mine = st1.at[tick, slot]

        @pl.loop(1, 16)
        def _(k):
            put(mine, mine, s1_s.at[tick], s1_r.at[tick], plane(k)[1])

    def merged(ref, tick):
        stats = ref[tick]
        teach_max = stats[:, 0, :]
        stud_max = stats[:, 3, :]
        top_teach = jnp.max(teach_max, axis=0, keepdims=True)
        top_stud = jnp.max(stud_max, axis=0, keepdims=True)
        teach_scale = jnp.exp(teach_max - top_teach)
        teach_sum = jnp.sum(stats[:, 1, :] * teach_scale, axis=0, keepdims=True)
        cross = jnp.sum(stats[:, 2, :] * teach_scale, axis=0, keepdims=True)
        stud_sum = jnp.sum(stats[:, 4, :] * jnp.exp(stud_max - top_stud), axis=0, keepdims=True)
        return top_teach, teach_sum, cross, top_stud, stud_sum

    def do_merge(tick):
        take(st1.at[tick, pl.ds(0, 15)], s1_r.at[tick])
        slot = z * 2 + c
        for i, row in enumerate(merged(st1, tick)):
            st2[tick, slot, i : i + 1, :] = row
        for i in range(5, 8):
            st2[tick, slot, i : i + 1, :] = jnp.zeros((1, 128), F32)
        mine = st2.at[tick, slot]

        @pl.loop(1, 16)
        def _(k):
            put(mine, mine, s2_s.at[tick], s2_r.at[tick], pillar(k))

    def do_finish(tick):
        take(st2.at[tick, pl.ds(0, 15)], s2_r.at[tick])
        teach_max, teach_sum, cross, stud_max, stud_sum = merged(st2, tick)
        div_out[pl.ds(tick, 1), :] = (
            cross / teach_sum - teach_max - jnp.log(teach_sum) + stud_max + jnp.log(stud_sum)
        )

    def do_spread(section):
        fresh = jnp.logical_and(first, section == DOWN)

        @pl.when(jnp.logical_not(fresh))
        def _():
            fin[section, :, pl.ds(fcol, COLS)] = xb[section, TICKS, pl.ds(frow, ROWS), :]
            for j in range(1, FS):
                p = lax.rem(f + j, FS)
                put(
                    xb.at[section, TICKS, pl.ds(pl.multiple_of(p * ROWS, ROWS), ROWS), :],
                    fin.at[section, :, pl.ds(fcol, COLS)], f_s.at[section], f_r.at[section], (s, p),
                )

        @pl.when(fresh)
        def _():
            fresh_copy = pltpu.make_async_copy(new_ref.at[TICKS - 1], fin.at[DOWN], local_h.at[2])
            fresh_copy.start()
            fresh_copy.wait()

    @pl.loop(0, STEPS)
    def _(i):
        code = jnp.int32(0)
        for k in range(STEPS):
            code = jnp.where(i == k, codes[k], code)
        kind = lax.div(code, 8)
        section = lax.rem(lax.div(code, 4), 2)
        tick = lax.rem(code, 4)

        pl.when(kind == SEND_DOWN)(functools.partial(do_send, DOWN, section, tick))
        pl.when(kind == SEND_UP)(functools.partial(do_send, UP, section, tick))
        pl.when(kind == HEAD)(functools.partial(do_head, section, tick))
        pl.when(kind == REDUCE)(functools.partial(do_reduce, section, tick))
        pl.when(kind == OUT)(functools.partial(do_out, section, tick))
        pl.when(kind == FORWARD)(functools.partial(do_forward, tick))
        pl.when(kind == SHARE)(functools.partial(do_share, tick))
        pl.when(kind == LOGITS)(functools.partial(do_logits, tick))
        pl.when(kind == MERGE)(functools.partial(do_merge, tick))
        pl.when(kind == FINISH)(functools.partial(do_finish, tick))
        pl.when(kind == SPREAD)(functools.partial(do_spread, section))

    @pl.when(jnp.logical_not(first))
    def _():
        take(fin.at[DOWN, :, pl.ds(0, D - COLS)], f_r.at[DOWN])
        take(fin.at[DOWN, :, pl.ds(0, D - COLS)], f_s.at[DOWN])

    take(fin.at[UP, :, pl.ds(0, D - COLS)], f_r.at[UP])
    take(fin.at[UP, :, pl.ds(0, D - COLS)], f_s.at[UP])
    down_out[0] = fin[DOWN]
    up_out[0] = fin[UP]

    @pl.loop(0, 2)
    def _(i):
        take(pw.at[i, :, pl.ds(0, 896)], w_s.at[i])

        @pl.when(follows(i)[0])
        def _():
            take(ow.at[i, pl.ds(0, 896), :], w_s.at[2 + i])

        @pl.when(jnp.logical_not(follows(i)[0]))
        def _():
            take(ow.at[i], w_s.at[2 + i])

        take(xb.at[i, 0, pl.ds(0, 112), :], x_s.at[i])

    @pl.when(first)
    def _():
        @pl.loop(2, 4)
        def _(i):
            take(xb.at[DOWN, 0, pl.ds(0, 112), :], x_s.at[i])

    @pl.loop(0, TICKS)
    def _(tick):
        for section in range(2):
            take(parts.at[section, tick, pl.ds(0, FS - 1)], rs_s.at[section, tick])
            inside = follows(section)[0]

            @pl.when(inside)
            def _():
                take(hv.at[section, tick, pl.ds(0, 112), :], ag_s.at[section, tick])

            @pl.when(jnp.logical_not(inside))
            def _():
                take(hv.at[section, tick], ag_s.at[section, tick])
                take(xp.at[section, tick], hop_s.at[section, tick])

        @pl.when(first)
        def _():
            take(xo.at[tick, pl.ds(0, 96), :], z_s.at[tick, 0])

            @pl.loop(1, 8)
            def _(k):
                take(xo.at[tick], z_s.at[tick, k])

        take(hid.at[tick, pl.ds(qrow, 32), pl.ds(0, D - COLS)], pl_s.at[tick, 0])
        take(hid.at[tick, pl.ds(orow, 32), :], pl_s.at[tick, 1])
        take(hid.at[tick, pl.ds(crow, 64), :], d2_s.at[tick])
        take(st1.at[tick, pl.ds(0, 15)], s1_s.at[tick])
        take(st2.at[tick, pl.ds(0, 15)], s2_s.at[tick])


def hand_over(*refs):
    count = len(refs) // 2
    for i in range(count):
        refs[count + i][...] = refs[i][...]


def local(
    new_batches, down_state, up_state, gains, w_value, w_out, final_gain, lm_head, teacher_logits
):
    hbm = pl.BlockSpec(memory_space=pl.ANY)
    vmem = pl.BlockSpec(memory_space=pltpu.VMEM)
    dma = pltpu.SemaphoreType.DMA
    down, up, logits, divergence = pl.pallas_call(
        kernel,
        out_shape=(
            jax.ShapeDtypeStruct((1, ROWS, D), BF),
            jax.ShapeDtypeStruct((1, ROWS, D), BF),
            jax.ShapeDtypeStruct((TICKS * MB, VOC), BF),
            jax.ShapeDtypeStruct((TICKS, MB), F32),
        ),
        in_specs=[hbm, hbm, hbm, hbm, hbm, hbm, hbm, hbm, hbm],
        out_specs=(vmem, vmem, vmem, vmem),
        scratch_shapes=[
            pltpu.VMEM((2, COLS, H), BF),
            pltpu.VMEM((2, H, COLS), BF),
            pltpu.VMEM((2, TICKS + 1, MB, COLS), BF),
            pltpu.VMEM((2, TICKS, MB, COLS), BF),
            pltpu.VMEM((2, TICKS, MB, WIDE), BF),
            pltpu.VMEM((2, TICKS, FS, ROWS, WIDE), BF),
            pltpu.VMEM((2, TICKS, ROWS, H), BF),
            pltpu.VMEM((2, TICKS, MB, H), BF),
            pltpu.VMEM((TICKS, MB, COLS), BF),
            pltpu.VMEM((TICKS, MB, D), BF),
            pltpu.VMEM((MB, D), BF),
            pltpu.VMEM((MB, VOC), F32),
            pltpu.VMEM((D, VOC), BF),
            pltpu.VMEM((TICKS * MB, VOC), BF),
            pltpu.VMEM((MB, 128), F32),
            pltpu.VMEM((TICKS, 16, 8, 128), F32),
            pltpu.VMEM((TICKS, 16, 8, 128), F32),
            pltpu.VMEM((2, ROWS, D), BF),
            pltpu.VMEM((1, 2, D), F32),
            pltpu.VMEM((1, D), F32),
            dma((4,)), dma((4,)), dma((5,)),
            dma((4,)), dma((4,)), dma((4,)), dma((4,)),
            dma((2, TICKS)), dma((2, TICKS)), dma((2, TICKS)), dma((2, TICKS)),
            dma((2, TICKS)), dma((2, TICKS)),
            dma((TICKS, 8)), dma((TICKS,)),
            dma((TICKS, 2)), dma((TICKS, 2)),
            dma((TICKS,)), dma((TICKS,)),
            dma((TICKS,)), dma((TICKS,)), dma((TICKS,)), dma((TICKS,)),
            dma((2,)), dma((2,)),
        ],
        compiler_params=pltpu.CompilerParams(
            collective_id=0, has_side_effects=True, vmem_limit_bytes=VMEM_LIMIT
        ),
        name="ticks_and_loss",
    )(
        new_batches, down_state, up_state, gains, w_value, w_out,
        final_gain.reshape(1, D), lm_head, teacher_logits,
    )
    whole = (down, up, logits, divergence)
    down, up, logits, divergence = pl.pallas_call(
        hand_over,
        out_shape=tuple(jax.ShapeDtypeStruct(one.shape, one.dtype) for one in whole),
        in_specs=[vmem] * 4,
        out_specs=(vmem,) * 4,
        compiler_params=pltpu.CompilerParams(vmem_limit_bytes=VMEM_LIMIT),
        name="hand_over",
    )(*whole)
    return (down, up, logits, divergence.reshape(TICKS * MB))


def solution(mesh):
    placed = (
        P(None, "fsdp", None),
        P("segment", "fsdp", None),
        P("segment", "fsdp", None),
        P("segment", None, None),
        P("segment", None, None, "fsdp"),
        P("segment", None, "fsdp", None),
        P(),
        P(None, ("segment", "fsdp")),
        P(None, ("segment", "fsdp")),
    )
    return jax.shard_map(
        local,
        mesh=mesh,
        in_specs=placed,
        out_specs=(
            P("segment", "fsdp", None),
            P("segment", "fsdp", None),
            P(None, ("segment", "fsdp")),
            P(),
        ),
        check_vma=False,
    )
```

time: 990 us -> 160 us (0.16)
  waiting for transfers between devices: 753 us -> 0 us
  Pallas kernels: 0 us -> 159 us
  blocking collectives: 150 us -> 0 us
  matrix products: 26.3 us -> 0 us
  other arithmetic: 25.9 us -> 0 us
  starting transfers between devices: 15.4 us -> 0 us
  between operations: 14.3 us -> 0.64 us
    psum x4 -> x0, waiting for transfers between devices: 545 us -> none  [the longest x3 338 us: local(): lax.psum(project_rows(down_rows, gain_pair[0], value_pair[0], out_pair[0]...]
    pallas_call x0 -> x2, Pallas kernels: none -> 159 us  [the longest x1 158 us: local(): pl.pallas_call(kernel, out_shape=(jax.ShapeDtypeStruct((1, ROWS, D), BF),...]
    all_gather x3 -> x0, waiting for transfers between devices: 146 us -> none  [the longest x1 54.9 us: local(): lax.all_gather(down_state[0], 'fsdp', axis=0, tiled=True)]
    pmax x1 -> x0, blocking collectives: 77.8 us -> none  [local(): lax.pmax((teach_max, stud_max), ('segment', 'fsdp'))]
    psum x1 -> x0, blocking collectives: 72.7 us -> none  [local(): lax.psum((teach_sum * teach_scale, cross_sum * teach_scale, stud_sum * jn...]
    ppermute x6 -> x0, waiting for transfers between devices: 60.5 us -> none  [from_behind(): lax.ppermute(value, axis, [(source, source + steps) for source in range(f...]
    dot_general x7 -> x0, matrix products: 26.3 us -> none  [the longest x6 21.3 us: project_rows(): return jnp.dot(head_values, out_proj, preferred_element_type=jnp.float32)]
    ppermute x6 -> x0, starting transfers between devices: 15.1 us -> none  [from_behind(): lax.ppermute(value, axis, [(source, source + steps) for source in range(f...]
  transfers between devices with their start and end apart: 13 -> 0, of which waited for: 12 -> 0; matrix products, arithmetic and copies ran while one was open for 2% -> 0% of each run, Pallas kernels for 0% -> 0%
where the time goes in v1:
time: 160 us
  Pallas kernels  159 us (99%)
    pallas_call x1, Pallas kernels, local(): pl.pallas_call(kernel, out_shape=(jax.ShapeDtypeStruct((1, ROWS, D), BF),...  158 us

profile of v1, /device:TPU:1, one launch (start us, length us, event | category | flops | bytes accessed | tf_op | source)
XLA Modules:
  0.0 160.1 jit_solution(18342035321372435682)
XLA Ops:
  0.6 157.5 %ticks_and_loss.1 = (bf16[1,16,4096]{2,1,0:T(8,128)(2,1)}, bf16[1,16,4096]{2,1,0:T(8,128)(2,1)}, bf16[384,512]{1,0:T(8,128)(2,1)}, f32[3,128]{1,0:T(4,128)}) custom-call(bf16[3,16,4096]{2,1,0:T(8,128)(2,1)} %new_ref.1, bf16[1,16,4096]{2,1,0:T(8,128)(2,1)} %down_ref.1, bf16[1,16,4096]{2,1,0:T(8,128)(2,1)} %up_ref.1, f32[1,2,4096]{2,1,0:T(2,128)} %gain_ref.1, ...), custom_call_target="tpu_custom_call" | custom-call | tf_op jit(solution)/shard_map/ticks_and_loss/pallas_call | solution.py:568
  158.1 2.0 %hand_over.1 = (bf16[1,16,4096]{2,1,0:T(8,128)(2,1)}, bf16[1,16,4096]{2,1,0:T(8,128)(2,1)}, bf16[384,512]{1,0:T(8,128)(2,1)}, f32[3,128]{1,0:T(4,128)}) custom-call(bf16[1,16,4096]{2,1,0:T(8,128)(2,1)} %get-tuple-element.12.refs_0_, bf16[1,16,4096]{2,1,0:T(8,128)(2,1)} %get-tuple-element.13.refs_1_, bf16[384,512]{1,0:T(8,128)(2,1)} %get-tuple-element.14.refs_2_, ...), custom_call_target="tpu_custom_call" | custom-call | tf_op jit(solution)/shard_map/hand_over/pallas_call | solution.py:618

commit v2 on v1

--- a/solution.py
+++ b/solution.py
@@ -79,7 +79,7 @@
 def kernel(
     new_ref, down_ref, up_ref, gain_ref, value_ref, out_ref, final_ref, head_ref, teach_ref,
     down_out, up_out, logit_out, div_out,
-    pw, ow, xb, xp, part, parts, hvo, hv, xo, hid, hn, acc, head, teach, cols, st1, st2, fin,
+    pw, ow, xb, xp, part, parts, hvo, hv, xo, hid, hn, acc, head, teach, heavy, known, cols, st1, st2, fin,
     gain, final, local_w, local_x, local_h,
     w_s, w_r, x_s, x_r, rs_s, rs_r, ag_s, ag_r, hop_s, hop_r, z_s, z_r, pl_s, pl_r, d2_s, d2_r,
     s1_s, s1_r, s2_s, s2_r, f_s, f_r,
@@ -233,6 +233,20 @@
             send_states(2 + i, new_ref, i, DOWN, 1 + i)
 
     gain_copy.wait()
+    teach_copy.wait()
+
+    @pl.loop(0, TICKS * MB // 32)
+    def _(i):
+        row = pl.multiple_of(i * 32, 32)
+        taught = teach[pl.ds(row, 32), :].astype(F32)
+        teach_max = jnp.max(taught, axis=-1, keepdims=True)
+        weight = jnp.exp(taught - teach_max)
+        heavy[pl.ds(row, 32), :] = weight
+        lane = lax.broadcasted_iota(jnp.int32, (32, 128), 1)
+        known[pl.ds(row, 32), :] = jnp.where(
+            lane == 0, teach_max, jnp.sum(weight, axis=-1, keepdims=True)
+        )
+
 
     codes = []
     for i in range(STEPS):
@@ -372,7 +386,6 @@
         @pl.when(tick == 0)
         def _():
             head_copy.wait()
-            teach_copy.wait()
             final_copy.wait()
 
         take(hid.at[tick, pl.ds(prow, 64), :], d2_r.at[tick])
@@ -384,14 +397,7 @@
             scale = lax.rsqrt(jnp.mean(rows * rows, axis=-1, keepdims=True) + EPS)
             hn[pl.ds(row, 16), :] = (rows * scale * final[...]).astype(BF)
 
-        acc[...] = jnp.zeros_like(acc)
-
-        @pl.loop(0, 4)
-        def _(k):
-            deep = pl.multiple_of(k * 1024, 1024)
-            acc[...] += jnp.dot(
-                hn[:, pl.ds(deep, 1024)], head[pl.ds(deep, 1024), :], preferred_element_type=F32
-            )
+        acc[...] = jnp.dot(hn[...], head[...], preferred_element_type=F32)
 
         @pl.loop(0, 4)
         def _(i):
@@ -400,15 +406,11 @@
             logits = acc[pl.ds(row, 32), :]
             logit_out[pl.ds(there, 32), :] = logits.astype(BF)
             taught = teach[pl.ds(there, 32), :].astype(F32)
-            teach_max = jnp.max(taught, axis=-1, keepdims=True)
-            weight = jnp.exp(taught - teach_max)
-            teach_sum = jnp.sum(weight, axis=-1, keepdims=True)
-            cross = jnp.sum(weight * (taught - logits), axis=-1, keepdims=True)
+            cross = jnp.sum(heavy[pl.ds(there, 32), :] * (taught - logits), axis=-1, keepdims=True)
             stud_max = jnp.max(logits, axis=-1, keepdims=True)
             stud_sum = jnp.sum(jnp.exp(logits - stud_max), axis=-1, keepdims=True)
             lane = lax.broadcasted_iota(jnp.int32, (32, 128), 1)
-            packed = jnp.where(lane == 0, teach_max, stud_max)
-            packed = jnp.where(lane == 1, teach_sum, packed)
+            packed = jnp.where(lane < 2, known[pl.ds(there, 32), :], stud_max)
             packed = jnp.where(lane == 2, cross, packed)
             packed = jnp.where(lane == 4, stud_sum, packed)
             cols[pl.ds(row, 32), :] = packed
@@ -590,6 +592,8 @@
             pltpu.VMEM((MB, VOC), F32),
             pltpu.VMEM((D, VOC), BF),
             pltpu.VMEM((TICKS * MB, VOC), BF),
+            pltpu.VMEM((TICKS * MB, VOC), F32),
+            pltpu.VMEM((TICKS * MB, 128), F32),
             pltpu.VMEM((MB, 128), F32),
             pltpu.VMEM((TICKS, 16, 8, 128), F32),
             pltpu.VMEM((TICKS, 16, 8, 128), F32),

time: 160 us -> 160 us (level)
  no operation moved by 1% of the time
where the time goes in v2:
time: 160 us
  Pallas kernels  160 us (100%)
    pallas_call x1, Pallas kernels, local(): pl.pallas_call(kernel, out_shape=(jax.ShapeDtypeStruct((1, ROWS, D), BF),...  158 us

profile of v2, /device:TPU:1, one launch (start us, length us, event | category | flops | bytes accessed | tf_op | source)
XLA Modules:
  0.0 160.4 jit_solution(16780216596134319024)
XLA Ops:
  0.6 157.7 %ticks_and_loss.1 = (bf16[1,16,4096]{2,1,0:T(8,128)(2,1)}, bf16[1,16,4096]{2,1,0:T(8,128)(2,1)}, bf16[384,512]{1,0:T(8,128)(2,1)}, f32[3,128]{1,0:T(4,128)}) custom-call(bf16[3,16,4096]{2,1,0:T(8,128)(2,1)} %new_ref.1, bf16[1,16,4096]{2,1,0:T(8,128)(2,1)} %down_ref.1, bf16[1,16,4096]{2,1,0:T(8,128)(2,1)} %up_ref.1, f32[1,2,4096]{2,1,0:T(2,128)} %gain_ref.1, ...), custom_call_target="tpu_custom_call" | custom-call | tf_op jit(solution)/shard_map/ticks_and_loss/pallas_call | solution.py:570
  158.4 2.0 %hand_over.1 = (bf16[1,16,4096]{2,1,0:T(8,128)(2,1)}, bf16[1,16,4096]{2,1,0:T(8,128)(2,1)}, bf16[384,512]{1,0:T(8,128)(2,1)}, f32[3,128]{1,0:T(4,128)}) custom-call(bf16[1,16,4096]{2,1,0:T(8,128)(2,1)} %get-tuple-element.12.refs_0_, bf16[1,16,4096]{2,1,0:T(8,128)(2,1)} %get-tuple-element.13.refs_1_, bf16[384,512]{1,0:T(8,128)(2,1)} %get-tuple-element.14.refs_2_, ...), custom_call_target="tpu_custom_call" | custom-call | tf_op jit(solution)/shard_map/hand_over/pallas_call | solution.py:622
